TPU v7x, 32 devices: a whole 2x2x4 slice. The times are simulated.
32 devices in a mesh: section: 8 (over z, x), fsdp: 4 (over y, core).
Axes of the slice: x: 2, y: 2, z: 4, core: 2. Of those that a mesh axis runs over, the one named last changes fastest.
Arguments:
- hidden: bfloat16 [2, 8, 512, 256], P(None, 'section', 'fsdp'), may hold values from -6 to 6
- grad_out: bfloat16 [2, 8, 512, 4096], P(None, 'section', 'fsdp'), may hold values from -0.375 to 0.375
- live_cols: int32 [8], replicated, may hold values from 128 to 256, as said below
- tok_count: int32 [2, 4], P(None, 'fsdp'), may hold values from 1 to 128, 384 in all within a row
Outputs:
- grad_down_t: float32 [8, 4096, 256], P('section', 'fsdp')
Inputs may be any that keep to these rules, and one draw needn't show every extreme that they name: `live_cols`: each entry is a multiple of 128; some section has all 256 hidden units live. `tok_count`: each direction's counts sum to 384, and some device of each direction holds 128 live tokens.
All inputs are finite; a program needn't handle non-finite values.
Results may differ from a plain program's by a relative error of at most 0.0003.
Values sent between devices are 32-bit elements; how exact they have to be, the bound alone decides.
A program may use at most 64 MiB of HBM per device.

v0:
```python
import jax
import jax.numpy as jnp
from jax import lax
from jax.sharding import PartitionSpec as P


def dense_term(cotangent, masked_rows):
    return lax.dot_general(
        cotangent, masked_rows, (((0,), (0,)), ((), ())), preferred_element_type=jnp.float32
    )


def mirror(shard_sum):
    section_count = lax.axis_size("section")
    pieces = shard_sum.reshape(section_count, -1)
    spread_out = lax.all_to_all(pieces, "section", split_axis=0, concat_axis=0, tiled=True)
    flipped = spread_out[::-1]
    collected = lax.all_to_all(flipped, "section", split_axis=0, concat_axis=0, tiled=True)
    return collected.reshape(shard_sum.shape)


def on_device(hidden, grad_out, live_cols, tok_count):
    section_count = lax.axis_size("section")
    own_index = lax.axis_index("section")
    far_index = section_count - 1 - own_index
    live_own = lax.dynamic_index_in_dim(live_cols, own_index, 0, keepdims=False)
    live_far = lax.dynamic_index_in_dim(live_cols, far_index, 0, keepdims=False)
    live_counts = jnp.stack([live_own, live_far])
    tok_rows = hidden.shape[2]
    hidden_width = hidden.shape[3]
    positions = lax.broadcasted_iota(jnp.int32, (2, tok_rows, hidden_width), 1)
    column_ids = lax.broadcasted_iota(jnp.int32, (2, tok_rows, hidden_width), 2)
    keep_mask = (positions < tok_count[:, 0][:, None, None]) & (
        column_ids < live_counts[:, None, None]
    )
    masked = jnp.where(keep_mask, hidden[:, 0], jnp.zeros_like(hidden[:, 0]))
    cotangent = grad_out[:, 0]

    def term_for(direction):
        return dense_term(cotangent[direction], masked[direction])

    summed = lax.psum_scatter(
        jnp.concatenate([term_for(0), term_for(1)], axis=1), "fsdp", scatter_dimension=0, tiled=True
    )
    own_part = summed[:, :hidden_width]
    far_part = mirror(summed[:, hidden_width:])
    return (own_part + far_part)[None]


def solution(mesh):
    in_specs = (
        P(None, "section", "fsdp", None),
        P(None, "section", "fsdp", None),
        P(),
        P(None, "fsdp"),
    )
    out_specs = P("section", "fsdp", None)
    return jax.shard_map(
        on_device, mesh=mesh, in_specs=in_specs, out_specs=out_specs, check_vma=False
    )
```

profile of v0, /device:TPU:8, one launch (start us, length us, event | category | flops | bytes accessed | tf_op | source)
XLA Modules:
  0.0 170.2 jit_solution(7742912622772124009)
XLA Ops:
  6.5 0.0 copy-start
  6.5 0.0 reduce-scatter.2.cloned.1.call-start
  6.5 1.5 fusion.7
  8.0 1.4 pad_add_fusion
  9.4 1.0 fusion.6
  10.5 2.0 %convolution_bitcast_fusion = f32[4096,256]{0,1:T(8,128)S(1)} fusion(bf16[2,1,128,4096]{3,2,1,0:T(8,128)(2,1)} %param.5, bf16[2,128,256]{2,1,0:T(8,128)(2,1)S(1)} %fusion.6), kind=kOutput, calls=%fused_computation.1 | convolution fusion | flops 268435456 | bytes 5308416 | tf_op jit(solution)/shard_map/dot_general | solution.py:8
  12.4 0.0 copy-done
  12.4 0.7 convolution_bitcast_fusion.1
  13.2 3.8 %pad_maximum_fusion = f32[4096,512]{0,1:T(8,128)} fusion(f32[4096,256]{0,1:T(8,128)S(1)} %convolution_bitcast_fusion, f32[4096,256]{0,1:T(8,128)S(1)} %convolution_bitcast_fusion.1), kind=kLoop, calls=%fused_computation | loop fusion | flops 2097152 | bytes 16777216 | tf_op jit(solution)/shard_map/concatenate | solution.py:43
  16.9 0.0 reduce-scatter.2.cloned.1.call-update
  16.9 73.0 %reduce-scatter.2.cloned.1.call-done = f32[1024,512]{0,1:T(8,128)} async-done(((f32[4096,512]{0,1:T(8,128)}), f32[1024,512]{0,1:T(8,128)}) %reduce-scatter.2.cloned.1.call-update) | async-done | bytes 2097168 | tf_op jit(solution)/shard_map/reduce_scatter | solution.py:42
  90.0 1.3 slice.29
  91.3 0.3 copy.9
  91.6 1.1 all_to_all.19
  92.7 30.7 %all_to_all.22 = f32[8,1,32768]{2,1,0:T(1,128)S(1)} all-to-all(f32[8,1,32768]{2,1,0:T(1,128)S(1)} %all_to_all.19), channel_id=1, replica_groups=mesh['section'=8,'fsdp'=4] {'section'}, dimensions={0} | all-to-all | bytes 2097152 | tf_op jit(solution)/shard_map/all_to_all | solution.py:16
  123.4 0.6 copy.16
  124.0 3.8 %rev.3 = f32[8,32768]{1,0:T(8,128)S(1)} reverse(f32[8,32768]{1,0:T(8,128)S(1)} %bitcast.25), dimensions={0} | reverse | bytes 2097152 | tf_op jit(solution)/shard_map/rev | solution.py:17
  127.8 1.1 copy.11
  128.9 28.8 %all_to_all.23 = f32[8,1,32768]{2,1,0:T(1,128)S(1)} all-to-all(f32[8,1,32768]{2,1,0:T(1,128)S(1)} %copy.11), channel_id=1, replica_groups=mesh['section'=8,'fsdp'=4] {'section'}, dimensions={0} | all-to-all | bytes 2097152 | tf_op jit(solution)/shard_map/all_to_all | solution.py:18
  157.7 2.5 %reduce = f32[8,32768]{1,0:T(8,128)S(1)} reduce(f32[8,1,32768]{2,1,0:T(1,128)S(1)} %all_to_all.23, f32[]{:T(128)} %constant.23), dimensions={1}, to_apply=%all_to_all.18.reduce_sub_computation | reduce | bytes 2097156 | tf_op jit(solution)/shard_map/all_to_all | solution.py:18
  160.2 0.2 reshape.16
  160.4 0.3 copy.12
  160.7 1.4 fusion
  162.1 1.3 copy.13
Async XLA Ops:
  6.5 5.9 %copy-start = (bf16[2,1,128,4096]{3,2,1,0:T(8,128)(2,1)S(1)}, bf16[2,1,128,4096]{3,2,1,0:T(8,128)(2,1)}, u32[]{:S(2)}) copy-start(bf16[2,1,128,4096]{3,2,1,0:T(8,128)(2,1)} %param.5) | copy-start | bytes 6291460
  6.5 83.4 %reduce-scatter.2.cloned.1.call-start = ((), (), s32[]{:S(2)}) async-start(), calls=%async_computation.3 | async-start | bytes 10485760 | tf_op jit(solution)/shard_map/reduce_scatter | solution.py:42
Sparse Core Ops, SparseCore 0:
  17.1 72.8 reduce-scatter.1
where the time goes:
time: 173 us; the launch traced here: 170 us
  waiting for transfers between devices  73 us (42%)
  blocking collectives  59.5 us (34%)
  between operations  13.5 us (8%)
  local copies, waits for them, and re-layouts  11.5 us (7%)
  other arithmetic  10.1 us (6%)
  matrix products  2.67 us (2%)
    reduce_scatter x1, waiting for transfers between devices, on_device(): lax.psum_scatter(jnp.concatenate([term_for(0), term_for(1)], axis=1), 'fs...  73 us
    all_to_all x1, blocking collectives, mirror(): lax.all_to_all(pieces, 'section', split_axis=0, concat_axis=0, tiled=True)  30.7 us
    all_to_all x1, blocking collectives, mirror(): lax.all_to_all(flipped, 'section', split_axis=0, concat_axis=0, tiled=True)  28.8 us
    rev x1, local copies, waits for them, and re-layouts, mirror(): flipped = spread_out[::-1]  3.81 us
    concatenate x1, other arithmetic, on_device(): jnp.concatenate([term_for(0), term_for(1)], axis=1)  3.76 us
  transfers between devices with their start and end apart: 1, of which 1 were waited for; matrix products, arithmetic and copies ran while one was open for 0% of the time, Pallas kernels for 0%

commit v1 on v0

v1 whole, which is shorter than its diff:
```python
import functools

import jax
import jax.numpy as jnp
from jax import lax
from jax.experimental import pallas as pl
from jax.experimental.pallas import tpu as pltpu
from jax.sharding import PartitionSpec as P

MESH = pl.DeviceIdType.MESH


def kernel(
    sections, chips, chunk, hidden, grads, live_cols, tok_count, out,
    mask_send, mask_recv, in_send, in_recv, own_mask, part_send, part_recv, far_send, far_recv,
    mask_ss, mask_rs, in_ss, in_rs, part_ss, part_rs, far_ss, far_rs,
):
    tokens, width = hidden.shape[2], hidden.shape[3]
    rows = out.shape[1]
    chunks = rows // chunk
    sec = lax.axis_index("section")
    rank = lax.axis_index("fsdp")
    chip, core = rank // 2, rank % 2
    sibling = {"section": sec, "fsdp": chip * 2 + (1 - core)}
    mirrored = {"section": sections - 1 - sec, "fsdp": rank}

    def peer(j):
        return {"section": sec, "fsdp": lax.rem(chip + j, chips) * 2 + core}

    barrier = pltpu.get_barrier_semaphore()
    for target in [sibling, mirrored] + [peer(j) for j in range(1, chips)]:
        pl.semaphore_signal(barrier, inc=1, device_id=target, device_id_type=MESH)

    def columns(j, c, k):
        block = lax.rem(chip + j, chips) * 2 + c
        return pl.ds(pl.multiple_of(block * rows + k * chunk, chunk), chunk)

    def mask_copy(d):
        return pltpu.make_async_remote_copy(
            mask_send.at[d], mask_recv.at[d], mask_ss.at[d], mask_rs.at[d],
            device_id=sibling, device_id_type=MESH)

    def in_copy(d, j, k):
        return pltpu.make_async_remote_copy(
            in_send.at[d, j, k], in_recv.at[d, j, k], in_ss.at[d, j, k], in_rs.at[d, j, k],
            device_id=sibling, device_id_type=MESH)

    def part_copy(d, j, k):
        return pltpu.make_async_remote_copy(
            part_send.at[d, j - 1, k], part_recv.at[d, j - 1, k],
            part_ss.at[d, j - 1, k], part_rs.at[d, j - 1, k],
            device_id=peer(j), device_id_type=MESH)

    def far_copy(k):
        return pltpu.make_async_remote_copy(
            far_send.at[k], far_recv.at[k], far_ss.at[k], far_rs.at[k],
            device_id=mirrored, device_id_type=MESH)

    positions = lax.broadcasted_iota(jnp.int32, (tokens, width), 0)
    column_ids = lax.broadcasted_iota(jnp.int32, (tokens, width), 1)
    live = (live_cols[sec], live_cols[sections - 1 - sec])
    order = [(k, j) for k in range(chunks) for j in list(range(1, chips)) + [0]]

    first = True
    for d in (1, 0):
        keep = (positions < tok_count[d, 0]) & (column_ids < live[d])
        masked = jnp.where(keep, hidden[d, 0].astype(jnp.float32), 0.0)
        mask_send[d] = masked
        own_mask[d, :tokens] = masked.astype(jnp.bfloat16)
        for k, j in order:
            in_send[d, j, k] = grads[d, 0, :, columns(j, 1 - core, k)].astype(jnp.float32)
            if first:
                pl.semaphore_wait(barrier, chips + 1)
                first = False
                mask_copy(d).start()
            elif (k, j) == order[0]:
                mask_copy(d).start()
            in_copy(d, j, k).start()

    def partial(d, j, k):
        in_copy(d, j, k).wait_recv()
        both = jnp.concatenate(
            [grads[d, 0, :, columns(j, core, k)], in_recv[d, j, k].astype(jnp.bfloat16)], axis=0)
        return lax.dot_general(
            both, own_mask[d], (((0,), (0,)), ((), ())), preferred_element_type=jnp.float32)

    def take_mask(d):
        mask_copy(d).wait_recv()
        own_mask[d, tokens:] = mask_recv[d].astype(jnp.bfloat16)

    def send_parts(d, k):
        for j in range(1, chips):
            part_send[d, j - 1, k] = partial(d, j, k)
            part_copy(d, j, k).start()

    take_mask(1)
    for k in range(chunks):
        send_parts(1, k)
        far_send[k] = partial(1, 0, k)
    take_mask(0)
    for k in range(chunks):
        total = far_send[k]
        for j in range(1, chips):
            part_copy(1, j, k).wait_recv()
            total = total + part_recv[1, j - 1, k]
        far_send[k] = total
        far_copy(k).start()
        send_parts(0, k)
        out[0, k * chunk:(k + 1) * chunk] = partial(0, 0, k)
    for k in range(chunks):
        here = slice(k * chunk, (k + 1) * chunk)
        total = out[0, here]
        for j in range(1, chips):
            part_copy(0, j, k).wait_recv()
            total = total + part_recv[0, j - 1, k]
        far_copy(k).wait_recv()
        out[0, here] = total + far_recv[k]
    for d in (1, 0):
        mask_copy(d).wait_send()
        for k, j in order:
            in_copy(d, j, k).wait_send()
            if j:
                part_copy(d, j, k).wait_send()
    for k in range(chunks):
        far_copy(k).wait_send()


def on_device(sections, ranks, hidden, grad_out, live_cols, tok_count):
    tokens, width = hidden.shape[2], hidden.shape[3]
    rows = grad_out.shape[3] // ranks
    chips = ranks // 2
    chunk = min(256, rows)
    chunks = rows // chunk
    f32 = jnp.float32
    dma = pltpu.SemaphoreType.DMA
    vmem = pl.BlockSpec(memory_space=pltpu.VMEM)
    smem = pl.BlockSpec(memory_space=pltpu.SMEM)
    return pl.pallas_call(
        functools.partial(kernel, sections, chips, chunk),
        out_shape=jax.ShapeDtypeStruct((1, rows, width), f32),
        in_specs=[vmem, vmem, smem, smem],
        out_specs=vmem,
        scratch_shapes=[
            pltpu.VMEM((2, tokens, width), f32),
            pltpu.VMEM((2, tokens, width), f32),
            pltpu.VMEM((2, chips, chunks, tokens, chunk), f32),
            pltpu.VMEM((2, chips, chunks, tokens, chunk), f32),
            pltpu.VMEM((2, 2 * tokens, width), jnp.bfloat16),
            pltpu.VMEM((2, chips - 1, chunks, chunk, width), f32),
            pltpu.VMEM((2, chips - 1, chunks, chunk, width), f32),
            pltpu.VMEM((chunks, chunk, width), f32),
            pltpu.VMEM((chunks, chunk, width), f32),
            dma((2,)), dma((2,)),
            dma((2, chips, chunks)), dma((2, chips, chunks)),
            dma((2, chips - 1, chunks)), dma((2, chips - 1, chunks)),
            dma((chunks,)), dma((chunks,)),
        ],
        compiler_params=pltpu.CompilerParams(
            collective_id=0, has_side_effects=True, vmem_limit_bytes=40 * 2**20),
        cost_estimate=pl.CostEstimate(
            flops=8 * tokens * rows * chips * width,
            bytes_accessed=4 * tokens * rows * ranks + 4 * rows * width, transcendentals=0),
    )(hidden, grad_out, live_cols, tok_count)


def solution(mesh):
    in_specs = (
        P(None, "section", "fsdp", None),
        P(None, "section", "fsdp", None),
        P(),
        P(None, "fsdp"),
    )
    out_specs = P("section", "fsdp", None)
    body = functools.partial(on_device, mesh.shape["section"], mesh.shape["fsdp"])
    return jax.shard_map(
        body, mesh=mesh, in_specs=in_specs, out_specs=out_specs, check_vma=False
    )
```

time: 173 us -> 65.2 us (0.38); the launches traced: 170 us -> 64.6 us
  waiting for transfers between devices: 73 us -> 0 us
  Pallas kernels: 0 us -> 59.7 us
  blocking collectives: 59.5 us -> 0 us
  between operations: 13.5 us -> 0.01 us
  other arithmetic: 10.1 us -> 0 us
  local copies, waits for them, and re-layouts: 11.5 us -> 4.86 us
  matrix products: 2.67 us -> 0 us
    reduce_scatter x1 -> x0, waiting for transfers between devices: 73 us -> none  [on_device(): lax.psum_scatter(jnp.concatenate([term_for(0), term_for(1)], axis=1), 'fs...]
    pallas_call x0 -> x1, Pallas kernels: none -> 59.7 us  [on_device(): pl.pallas_call(functools.partial(kernel, sections, chips, chunk), out_sha...]
    all_to_all x2 -> x0, blocking collectives: 59.5 us -> none  [the longest x1 30.7 us: mirror(): lax.all_to_all(pieces, 'section', split_axis=0, concat_axis=0, tiled=True)]
    unnamed x3 -> x8, local copies, waits for them, and re-layouts: 0.61 us -> 4.86 us
    rev x1 -> x0, local copies, waits for them, and re-layouts: 3.81 us -> none  [mirror(): flipped = spread_out[::-1]]
    concatenate x1 -> x0, other arithmetic: 3.76 us -> none  [on_device(): jnp.concatenate([term_for(0), term_for(1)], axis=1)]
    dot_general x2 -> x0, matrix products: 2.67 us -> none  [dense_term(): lax.dot_general(cotangent, masked_rows, (((0,), (0,)), ((), ())), preferr...]
    all_to_all x1 -> x0, other arithmetic: 2.49 us -> none  [mirror(): lax.all_to_all(flipped, 'section', split_axis=0, concat_axis=0, tiled=True)]
  transfers between devices with their start and end apart: 1 -> 0, of which waited for: 1 -> 0; matrix products, arithmetic and copies ran while one was open for 0% -> 0% of each run, Pallas kernels for 0% -> 0%
where the time goes in v1:
time: 65.2 us; the launch traced here: 64.6 us
  Pallas kernels  59.7 us (92%)
  local copies, waits for them, and re-layouts  4.86 us (7%)
    pallas_call x1, Pallas kernels, on_device(): pl.pallas_call(functools.partial(kernel, sections, chips, chunk), out_sha...  59.7 us
    unnamed x8, local copies, waits for them, and re-layouts  4.86 us

profile of v1, /device:TPU:8, one launch (start us, length us, event | category | flops | bytes accessed | tf_op | source)
XLA Modules:
  0.0 64.6 jit_solution(3621801405366004320)
XLA Ops:
  0.0 0.7 %copy.5.tok_count = s32[2,1]{1,0:T(2,128)S(1)} copy(s32[2,1]{0,1:T(1,128)} %param.7) | data formatting | bytes 16 | tf_op args[3]
  0.7 0.0 copy-start
  0.7 1.6 %copy-done = bf16[2,1,128,4096]{3,2,1,0:T(8,128)(2,1)S(1)} copy-done((bf16[2,1,128,4096]{3,2,1,0:T(8,128)(2,1)S(1)}, bf16[2,1,128,4096]{3,2,1,0:T(8,128)(2,1)}, u32[]{:S(2)}) %copy-start) | copy-done | bytes 2097176
  2.3 0.0 copy-start.1
  2.3 0.9 %copy-done.1 = bf16[2,1,128,256]{3,2,1,0:T(8,128)(2,1)S(1)} copy-done((bf16[2,1,128,256]{3,2,1,0:T(8,128)(2,1)S(1)}, bf16[2,1,128,256]{3,2,1,0:T(8,128)(2,1)}, u32[]{:S(2)}) %copy-start.1) | copy-done | bytes 131096
  3.2 0.0 copy-start.2
  3.2 0.7 %copy-done.2 = s32[8]{0:T(128)S(1)} copy-done((s32[8]{0:T(128)S(1)}, s32[8]{0:T(128)}, u32[]{:S(2)}) %copy-start.2) | copy-done | bytes 56
  3.9 59.7 %shard_map.46 = f32[1,1024,256]{2,1,0:T(8,128)S(1)} custom-call(bf16[2,1,128,256]{3,2,1,0:T(8,128)(2,1)S(1)} %copy-done.1, bf16[2,1,128,4096]{3,2,1,0:T(8,128)(2,1)S(1)} %copy-done, s32[8]{0:T(128)S(1)} %copy-done.2, s32[2,1]{1,0:T(2,128)S(1)} %copy.5.tok_count), custom_call_target="tpu_custom_call" | custom-call | flops 536870912 | bytes 3145728 | tf_op jit(solution)/shard_map/pallas_call | solution.py:138
  63.6 1.0 %copy.7 = f32[1,1024,256]{2,1,0:T(8,128)} copy(f32[1,1024,256]{2,1,0:T(8,128)S(1)} %shard_map.46) | data formatting | bytes 2097152
Async XLA Ops:
  0.7 1.6 %copy-start = (bf16[2,1,128,4096]{3,2,1,0:T(8,128)(2,1)S(1)}, bf16[2,1,128,4096]{3,2,1,0:T(8,128)(2,1)}, u32[]{:S(2)}) copy-start(bf16[2,1,128,4096]{3,2,1,0:T(8,128)(2,1)} %grads.1) | copy-start | bytes 6291460
  2.3 0.9 %copy-start.1 = (bf16[2,1,128,256]{3,2,1,0:T(8,128)(2,1)S(1)}, bf16[2,1,128,256]{3,2,1,0:T(8,128)(2,1)}, u32[]{:S(2)}) copy-start(bf16[2,1,128,256]{3,2,1,0:T(8,128)(2,1)} %hidden.1) | copy-start | bytes 393220
  3.2 0.7 %copy-start.2 = (s32[8]{0:T(128)S(1)}, s32[8]{0:T(128)}, u32[]{:S(2)}) copy-start(s32[8]{0:T(128)} %live_cols.1) | copy-start | bytes 100

commit v2 on v1

--- a/solution.py
+++ b/solution.py
@@ -11,11 +11,12 @@
 
 
 def kernel(
-    sections, chips, chunk, hidden, grads, live_cols, tok_count, out,
+    sections, chips, chunk, hidden_hbm, grads_hbm, live_hbm, tok_hbm, out,
+    hidden, grads, live_cols, tok_count, total, fetch_sem, out_sem,
     mask_send, mask_recv, in_send, in_recv, own_mask, part_send, part_recv, far_send, far_recv,
     mask_ss, mask_rs, in_ss, in_rs, part_ss, part_rs, far_ss, far_rs,
 ):
-    tokens, width = hidden.shape[2], hidden.shape[3]
+    tokens, width = hidden.shape[1], hidden.shape[2]
     rows = out.shape[1]
     chunks = rows // chunk
     sec = lax.axis_index("section")
@@ -56,91 +57,129 @@
             far_send.at[k], far_recv.at[k], far_ss.at[k], far_rs.at[k],
             device_id=mirrored, device_id_type=MESH)
 
+    def fetch(d):
+        return (
+            pltpu.make_async_copy(hidden_hbm.at[d, 0], hidden.at[d], fetch_sem.at[d]),
+            pltpu.make_async_copy(grads_hbm.at[d, 0], grads.at[d], fetch_sem.at[2 + d]))
+
+    counts = (
+        pltpu.make_async_copy(live_hbm, live_cols, fetch_sem.at[4]),
+        pltpu.make_async_copy(tok_hbm, tok_count, fetch_sem.at[5]))
+    for copy in counts + fetch(1) + fetch(0):
+        copy.start()
+    for copy in counts:
+        copy.wait()
     positions = lax.broadcasted_iota(jnp.int32, (tokens, width), 0)
     column_ids = lax.broadcasted_iota(jnp.int32, (tokens, width), 1)
     live = (live_cols[sec], live_cols[sections - 1 - sec])
     order = [(k, j) for k in range(chunks) for j in list(range(1, chips)) + [0]]
 
-    first = True
-    for d in (1, 0):
-        keep = (positions < tok_count[d, 0]) & (column_ids < live[d])
-        masked = jnp.where(keep, hidden[d, 0].astype(jnp.float32), 0.0)
+    def stage(d):
+        for copy in fetch(d):
+            copy.wait()
+        keep = (positions < tok_count[d]) & (column_ids < live[d])
+        masked = jnp.where(keep, hidden[d].astype(jnp.float32), 0.0)
         mask_send[d] = masked
         own_mask[d, :tokens] = masked.astype(jnp.bfloat16)
+        if d:
+            pl.semaphore_wait(barrier, chips + 1)
+        mask_copy(d).start()
         for k, j in order:
-            in_send[d, j, k] = grads[d, 0, :, columns(j, 1 - core, k)].astype(jnp.float32)
-            if first:
-                pl.semaphore_wait(barrier, chips + 1)
-                first = False
-                mask_copy(d).start()
-            elif (k, j) == order[0]:
-                mask_copy(d).start()
+            in_send[d, j, k] = grads[d, :, columns(j, 1 - core, k)].astype(jnp.float32)
             in_copy(d, j, k).start()
+
+    def take_mask(d):
+        mask_copy(d).wait_recv()
+        own_mask[d, tokens:] = mask_recv[d].astype(jnp.bfloat16)
 
     def partial(d, j, k):
         in_copy(d, j, k).wait_recv()
         both = jnp.concatenate(
-            [grads[d, 0, :, columns(j, core, k)], in_recv[d, j, k].astype(jnp.bfloat16)], axis=0)
+            [grads[d, :, columns(j, core, k)], in_recv[d, j, k].astype(jnp.bfloat16)], axis=0)
         return lax.dot_general(
             both, own_mask[d], (((0,), (0,)), ((), ())), preferred_element_type=jnp.float32)
-
-    def take_mask(d):
-        mask_copy(d).wait_recv()
-        own_mask[d, tokens:] = mask_recv[d].astype(jnp.bfloat16)
 
     def send_parts(d, k):
         for j in range(1, chips):
             part_send[d, j - 1, k] = partial(d, j, k)
             part_copy(d, j, k).start()
 
-    take_mask(1)
-    for k in range(chunks):
-        send_parts(1, k)
-        far_send[k] = partial(1, 0, k)
-    take_mask(0)
-    for k in range(chunks):
-        total = far_send[k]
+    def forward(k):
+        reduced = far_send[k]
         for j in range(1, chips):
             part_copy(1, j, k).wait_recv()
-            total = total + part_recv[1, j - 1, k]
-        far_send[k] = total
+            reduced = reduced + part_recv[1, j - 1, k]
+        far_send[k] = reduced
         far_copy(k).start()
+
+    lag = min(3, chunks)
+    stage(1)
+    take_mask(1)
+    for k in range(lag):
+        send_parts(1, k)
+    for k in range(lag):
+        far_send[k] = partial(1, 0, k)
+    stage(0)
+    for k in range(chunks):
+        forward(k)
+        if k + lag < chunks:
+            send_parts(1, k + lag)
+            far_send[k + lag] = partial(1, 0, k + lag)
+        else:
+            if k + lag == chunks:
+                take_mask(0)
+            send_parts(0, k + lag - chunks)
+    for k in range(lag, chunks):
         send_parts(0, k)
-        out[0, k * chunk:(k + 1) * chunk] = partial(0, 0, k)
-    for k in range(chunks):
-        here = slice(k * chunk, (k + 1) * chunk)
-        total = out[0, here]
+    for k in range(chunks):
+        total[k] = partial(0, 0, k)
+    for k in range(chunks):
+        reduced = total[k]
         for j in range(1, chips):
             part_copy(0, j, k).wait_recv()
-            total = total + part_recv[0, j - 1, k]
-        far_copy(k).wait_recv()
-        out[0, here] = total + far_recv[k]
+            reduced = reduced + part_recv[0, j - 1, k]
+        total[k] = reduced
     for d in (1, 0):
         mask_copy(d).wait_send()
         for k, j in order:
             in_copy(d, j, k).wait_send()
             if j:
                 part_copy(d, j, k).wait_send()
+
+    def store(k):
+        return pltpu.make_async_copy(
+            total.at[k], out.at[0, k * chunk:(k + 1) * chunk], out_sem.at[k])
+
+    for k in range(chunks):
+        far_copy(k).wait_recv()
+        total[k] += far_recv[k]
+        store(k).start()
     for k in range(chunks):
         far_copy(k).wait_send()
+        store(k).wait()
 
 
 def on_device(sections, ranks, hidden, grad_out, live_cols, tok_count):
     tokens, width = hidden.shape[2], hidden.shape[3]
     rows = grad_out.shape[3] // ranks
     chips = ranks // 2
-    chunk = min(256, rows)
+    chunk = min(128, rows)
     chunks = rows // chunk
     f32 = jnp.float32
     dma = pltpu.SemaphoreType.DMA
-    vmem = pl.BlockSpec(memory_space=pltpu.VMEM)
-    smem = pl.BlockSpec(memory_space=pltpu.SMEM)
+    hbm = pl.BlockSpec(memory_space=pltpu.HBM)
     return pl.pallas_call(
         functools.partial(kernel, sections, chips, chunk),
         out_shape=jax.ShapeDtypeStruct((1, rows, width), f32),
-        in_specs=[vmem, vmem, smem, smem],
-        out_specs=vmem,
+        in_specs=[hbm] * 4,
+        out_specs=hbm,
         scratch_shapes=[
+            pltpu.VMEM((2, tokens, width), jnp.bfloat16),
+            pltpu.VMEM((2, tokens, grad_out.shape[3]), jnp.bfloat16),
+            pltpu.SMEM(live_cols.shape, jnp.int32),
+            pltpu.SMEM((2,), jnp.int32),
+            pltpu.VMEM((chunks, chunk, width), f32),
+            dma((6,)), dma((chunks,)),
             pltpu.VMEM((2, tokens, width), f32),
             pltpu.VMEM((2, tokens, width), f32),
             pltpu.VMEM((2, chips, chunks, tokens, chunk), f32),
@@ -156,11 +195,11 @@
             dma((chunks,)), dma((chunks,)),
         ],
         compiler_params=pltpu.CompilerParams(
-            collective_id=0, has_side_effects=True, vmem_limit_bytes=40 * 2**20),
+            collective_id=0, has_side_effects=True, vmem_limit_bytes=48 * 2**20),
         cost_estimate=pl.CostEstimate(
             flops=8 * tokens * rows * chips * width,
             bytes_accessed=4 * tokens * rows * ranks + 4 * rows * width, transcendentals=0),
-    )(hidden, grad_out, live_cols, tok_count)
+    )(*(pltpu.with_memory_space_constraint(a, pltpu.HBM) for a in (hidden, grad_out, live_cols, tok_count.reshape(2))))
 
 
 def solution(mesh):

time: 65.2 us -> 59 us (0.905)
  local copies, waits for them, and re-layouts: 4.86 us -> 0.97 us
  Pallas kernels: 59.7 us -> 57.9 us
    unnamed x8 -> x1, local copies, waits for them, and re-layouts: 4.86 us -> 0.97 us
    pallas_call x1, Pallas kernels: 59.7 us -> 57.9 us  [on_device(): pl.pallas_call(functools.partial(kernel, sections, chips, chunk), out_sha...]
where the time goes in v2:
time: 59 us; the launch traced here: 58.9 us
  Pallas kernels  57.9 us (98%)
  local copies, waits for them, and re-layouts  0.97 us (2%)
    pallas_call x1, Pallas kernels, on_device(): pl.pallas_call(functools.partial(kernel, sections, chips, chunk), out_sha...  57.9 us

profile of v2, /device:TPU:8, one launch (start us, length us, event | category | flops | bytes accessed | tf_op | source)
XLA Modules:
  0.0 58.9 jit_solution(7614060978967384560)
XLA Ops:
  0.0 57.9 %shard_map.46 = f32[1,1024,256]{2,1,0:T(8,128)S(1)} custom-call(bf16[2,1,128,256]{3,2,1,0:T(8,128)(2,1)} %hidden_hbm.1, bf16[2,1,128,4096]{3,2,1,0:T(8,128)(2,1)} %grads_hbm.1, s32[8]{0:T(128)} %live_hbm.1, s32[2]{0:T(128)} %bitcast.1), custom_call_target="tpu_custom_call" | custom-call | flops 536870912 | bytes 3145728 | tf_op jit(solution)/shard_map/pallas_call | solution.py:171
  57.9 1.0 %copy.6 = f32[1,1024,256]{2,1,0:T(8,128)} copy(f32[1,1024,256]{2,1,0:T(8,128)S(1)} %shard_map.46) | data formatting | bytes 2097152

commit v3 on v2

--- a/solution.py
+++ b/solution.py
@@ -12,7 +12,7 @@
 
 def kernel(
     sections, chips, chunk, hidden_hbm, grads_hbm, live_hbm, tok_hbm, out,
-    hidden, grads, live_cols, tok_count, total, fetch_sem, out_sem,
+    hidden, grads, live_cols, tok_count, total, fetch_sem,
     mask_send, mask_recv, in_send, in_recv, own_mask, part_send, part_recv, far_send, far_recv,
     mask_ss, mask_rs, in_ss, in_rs, part_ss, part_rs, far_ss, far_rs,
 ):
@@ -84,7 +84,9 @@
         if d:
             pl.semaphore_wait(barrier, chips + 1)
         mask_copy(d).start()
-        for k, j in order:
+
+    def spread(d, blocks):
+        for k, j in blocks:
             in_send[d, j, k] = grads[d, :, columns(j, 1 - core, k)].astype(jnp.float32)
             in_copy(d, j, k).start()
 
@@ -112,14 +114,19 @@
         far_send[k] = reduced
         far_copy(k).start()
 
-    lag = min(3, chunks)
+    lag = min(2, chunks)
     stage(1)
+    spread(1, order[:chips])
+    spread(1, order[chips:2 * chips])
     take_mask(1)
-    for k in range(lag):
+    send_parts(1, 0)
+    spread(1, order[2 * chips:])
+    for k in range(1, lag):
         send_parts(1, k)
     for k in range(lag):
         far_send[k] = partial(1, 0, k)
     stage(0)
+    spread(0, order)
     for k in range(chunks):
         forward(k)
         if k + lag < chunks:
@@ -146,17 +153,11 @@
             if j:
                 part_copy(d, j, k).wait_send()
 
-    def store(k):
-        return pltpu.make_async_copy(
-            total.at[k], out.at[0, k * chunk:(k + 1) * chunk], out_sem.at[k])
-
     for k in range(chunks):
         far_copy(k).wait_recv()
-        total[k] += far_recv[k]
-        store(k).start()
+        out[0, k * chunk:(k + 1) * chunk] = total[k] + far_recv[k]
     for k in range(chunks):
         far_copy(k).wait_send()
-        store(k).wait()
 
 
 def on_device(sections, ranks, hidden, grad_out, live_cols, tok_count):
@@ -172,14 +173,14 @@
         functools.partial(kernel, sections, chips, chunk),
         out_shape=jax.ShapeDtypeStruct((1, rows, width), f32),
         in_specs=[hbm] * 4,
-        out_specs=hbm,
+        out_specs=pl.BlockSpec(memory_space=pltpu.VMEM),
         scratch_shapes=[
             pltpu.VMEM((2, tokens, width), jnp.bfloat16),
             pltpu.VMEM((2, tokens, grad_out.shape[3]), jnp.bfloat16),
             pltpu.SMEM(live_cols.shape, jnp.int32),
             pltpu.SMEM((2,), jnp.int32),
             pltpu.VMEM((chunks, chunk, width), f32),
-            dma((6,)), dma((chunks,)),
+            dma((6,)),
             pltpu.VMEM((2, tokens, width), f32),
             pltpu.VMEM((2, tokens, width), f32),
             pltpu.VMEM((2, chips, chunks, tokens, chunk), f32),

time: 59 us -> 58.8 us (level)
  no operation moved by 1% of the time
where the time goes in v3:
time: 58.8 us; the launch traced here: 58.6 us
  Pallas kernels  57.6 us (98%)
  local copies, waits for them, and re-layouts  0.97 us (2%)
    pallas_call x1, Pallas kernels, on_device(): pl.pallas_call(functools.partial(kernel, sections, chips, chunk), out_sha...  57.6 us

profile of v3, /device:TPU:8, one launch (start us, length us, event | category | flops | bytes accessed | tf_op | source)
XLA Modules:
  0.0 58.6 jit_solution(17002777454083238447)
XLA Ops:
  0.0 57.6 %shard_map.46 = f32[1,1024,256]{2,1,0:T(8,128)S(1)} custom-call(bf16[2,1,128,256]{3,2,1,0:T(8,128)(2,1)} %hidden_hbm.1, bf16[2,1,128,4096]{3,2,1,0:T(8,128)(2,1)} %grads_hbm.1, s32[8]{0:T(128)} %live_hbm.1, s32[2]{0:T(128)} %bitcast.1), custom_call_target="tpu_custom_call" | custom-call | flops 536870912 | bytes 3145728 | tf_op jit(solution)/shard_map/pallas_call | solution.py:172
  57.6 1.0 %copy.6 = f32[1,1024,256]{2,1,0:T(8,128)} copy(f32[1,1024,256]{2,1,0:T(8,128)S(1)} %shard_map.46) | data formatting | bytes 2097152

commit v4 on v3

--- a/solution.py
+++ b/solution.py
@@ -123,15 +123,16 @@
     spread(1, order[2 * chips:])
     for k in range(1, lag):
         send_parts(1, k)
-    for k in range(lag):
-        far_send[k] = partial(1, 0, k)
-    stage(0)
-    spread(0, order)
-    for k in range(chunks):
+    far_send[0] = partial(1, 0, 0)
+    for k in range(chunks):
+        if k:
+            far_send[k] = partial(1, 0, k)
         forward(k)
+        if k == 0:
+            stage(0)
+            spread(0, order)
         if k + lag < chunks:
             send_parts(1, k + lag)
-            far_send[k + lag] = partial(1, 0, k + lag)
         else:
             if k + lag == chunks:
                 take_mask(0)

time: 58.8 us -> 58.8 us (level)
  no operation moved by 1% of the time
where the time goes in v4:
time: 58.8 us; the launch traced here: 58.6 us
  Pallas kernels  57.6 us (98%)
  local copies, waits for them, and re-layouts  0.97 us (2%)
    pallas_call x1, Pallas kernels, on_device(): pl.pallas_call(functools.partial(kernel, sections, chips, chunk), out_sha...  57.6 us

profile of v4, /device:TPU:8, one launch (start us, length us, event | category | flops | bytes accessed | tf_op | source)
XLA Modules:
  0.0 58.6 jit_solution(17213054688017466373)
XLA Ops:
  0.0 57.6 %shard_map.46 = f32[1,1024,256]{2,1,0:T(8,128)S(1)} custom-call(bf16[2,1,128,256]{3,2,1,0:T(8,128)(2,1)} %hidden_hbm.1, bf16[2,1,128,4096]{3,2,1,0:T(8,128)(2,1)} %grads_hbm.1, s32[8]{0:T(128)} %live_hbm.1, s32[2]{0:T(128)} %bitcast.1), custom_call_target="tpu_custom_call" | custom-call | flops 536870912 | bytes 3145728 | tf_op jit(solution)/shard_map/pallas_call | solution.py:173
  57.6 1.0 %copy.6 = f32[1,1024,256]{2,1,0:T(8,128)} copy(f32[1,1024,256]{2,1,0:T(8,128)S(1)} %shard_map.46) | data formatting | bytes 2097152
